TPU v7x, 32 devices: a whole 2x2x4 slice. The times are simulated.
32 devices in a mesh: groups: 2 (over y), tok: 8 (over z, x), voc: 2 (over core).
Axes of the slice: x: 2, y: 2, z: 4, core: 2. Of those that a mesh axis runs over, the one named last changes fastest.
Arguments:
- teacher: bfloat16 [16, 48, 81920], P(('groups', 'tok'), None, 'voc'), parts along dimension 0, may hold values from 0.0009994507 to 1
- student: bfloat16 [48, 16, 65536], P('voc', 'groups', 'tok'), parts along dimension 1, may hold values from -8 to 284
- block_maps: bfloat16 [512, 2, 4, 128, 128], P('tok', 'voc'), may hold values from 0.0009994507 to 1
- slot_index: int32 [512, 2, 4], P('tok', 'voc'), may hold values from 0 to 39, as said below
- slot_count: int32 [512, 2], P('tok', 'voc'), may hold values from 0 to 4, as said below
Outputs:
- logit_grad: bfloat16 [48, 16, 65536], P('voc', 'groups', 'tok'), parts along dimension 1
- divergence: float32 [48, 16], P('voc', 'groups'), parts along dimension 1
There are 2 independent parts, one for each index of `groups`. A program takes and returns all parts, laid end to end along the dimension named above; an argument that names none is the same for every part. Nothing has to cross between parts.
Inputs may be any that keep to these rules, and one draw needn't show every extreme that they name: `slot_index`: within one student block and half the 4 indices are distinct. slot_count[s, 0] is at least 1 for every student block s.
All inputs are finite; a program needn't handle non-finite values.
Results may differ from a plain program's by a relative error of at most 0.0055.
Values may be sent and summed in bfloat16 or wider, within the bound.
A program may use at most 128 MiB of HBM per device.

v0:
```python
import jax
import jax.numpy as jnp
from jax import lax
from jax.sharding import PartitionSpec as P


def apply_maps(columns, matrices, indices, counts, span_blocks):
    slots_all = matrices.shape[1]
    blocks = matrices.shape[-1]
    student_blocks = matrices.shape[0]
    active = (jnp.arange(slots_all, dtype=jnp.int32)[None, :] < counts[:, None]).astype(jnp.float32)
    onehot = (
        indices[:, :, None] == jnp.arange(span_blocks, dtype=jnp.int32)[None, None, :]
    ).astype(jnp.float32)
    onehot = (onehot * active[:, :, None]).astype(jnp.bfloat16)
    lead = columns.shape[:-1]
    split_cols = columns.reshape(lead + (span_blocks, blocks))
    picked = jnp.einsum(
        "...ta,skt->...ska", split_cols, onehot, preferred_element_type=jnp.float32
    ).astype(jnp.bfloat16)
    result = jnp.einsum("...ska,skab->...sb", picked, matrices, preferred_element_type=jnp.float32)
    return result.reshape(lead + (student_blocks * blocks,))


def body(teacher, student, block_maps, slot_index, slot_count):
    shards = lax.axis_size("tok")
    row_count = teacher.shape[1]
    half_width = teacher.shape[2]
    blocks = block_maps.shape[-1]
    group_blocks = half_width // (shards * blocks)
    local_rows = teacher.reshape(row_count, shards, group_blocks * blocks)
    partial_map = apply_maps(
        lax.all_to_all(local_rows, "tok", split_axis=1, concat_axis=1, tiled=True),
        block_maps[:, 0],
        slot_index[:, 0],
        slot_count[:, 0],
        group_blocks,
    )
    mapped = lax.psum_scatter(
        partial_map.astype(jnp.bfloat16), "voc", scatter_dimension=0, tiled=True
    ).astype(jnp.float32)
    logit_f = student.astype(jnp.float32)
    local_top = jnp.max(logit_f, axis=-1)
    mass_local = jnp.sum(mapped, axis=-1)
    entropy_local = jnp.sum(mapped * jnp.log(mapped), axis=-1)
    cross_local = jnp.sum(mapped * logit_f, axis=-1)
    row_top = lax.pmax(local_top, "tok")
    shifted = jnp.exp(logit_f - row_top[..., None])
    exp_total, mass, entropy_part, cross_part = lax.psum(
        (jnp.sum(shifted, axis=-1), mass_local, entropy_local, cross_local), "tok"
    )
    divergence = (
        entropy_part / mass - jnp.log(mass) - cross_part / mass + row_top + jnp.log(exp_total)
    )
    vocab_words = shards * student.shape[2]
    logit_grad = (vocab_words * (shifted / exp_total[..., None] - mapped / mass[..., None])).astype(
        jnp.bfloat16
    )
    return (logit_grad, divergence)


def solution(mesh):
    return jax.shard_map(
        body,
        mesh=mesh,
        in_specs=(
            P(("groups", "tok"), None, "voc"),
            P("voc", "groups", "tok"),
            P("tok", "voc", None, None, None),
            P("tok", "voc", None),
            P("tok", "voc"),
        ),
        out_specs=(P("voc", "groups", "tok"), P("voc", "groups")),
        check_vma=False,
    )
```

profile of v0, /device:TPU:0, one launch (start us, length us, event | category | flops | bytes accessed | tf_op | source)
XLA Modules:
  0.0 284.6 jit_solution(8757600605543398018)
XLA Ops:
  7.2 4.3 %copy.30 = bf16[6,8,8,5120]{3,2,1,0:T(8,128)(2,1)S(1)} copy(bf16[6,8,8,5120]{3,1,2,0:T(8,128)(2,1)} %bitcast.43) | data formatting | bytes 7864320
  11.4 0.0 copy-start.2
  11.5 4.1 %copy.20 = bf16[48,8,5120]{2,0,1:T(8,128)(2,1)} copy(bf16[48,8,5120]{2,1,0:T(8,128)(2,1)S(1)} %bitcast.42) | data formatting | bytes 7864320 | tf_op jit(solution)/shard_map/reshape | solution.py:31
  15.5 0.0 copy-start.1
  15.5 7.4 %all-to-all-start = ((bf16[48,8,5120]{2,0,1:T(8,128)(2,1)}), bf16[48,8,5120]{2,0,1:T(8,128)(2,1)}, u32[]{:S(2)}, u32[]{:S(2)}) async-start(bf16[48,8,5120]{2,0,1:T(8,128)(2,1)} %copy.20), calls=%async_computation | async-start | bytes 7864320 | tf_op jit(solution)/shard_map/all_to_all | solution.py:33
  22.9 0.0 reduce-scatter.2.cloned.1.call-start
  22.9 0.0 copy-done.2
  23.0 87.6 %all-to-all-done = bf16[48,8,5120]{2,0,1:T(8,128)(2,1)} async-done(((bf16[48,8,5120]{2,0,1:T(8,128)(2,1)}), bf16[48,8,5120]{2,0,1:T(8,128)(2,1)}, u32[]{:S(2)}, u32[]{:S(2)}) %all-to-all-start) | async-done | bytes 3932192 | tf_op jit(solution)/shard_map/all_to_all | solution.py:33
  110.6 5.0 %copy.31 = bf16[48,8,40,128]{3,2,1,0:T(8,128)(2,1)} copy(bf16[48,8,40,128]{3,1,2,0:T(8,128)(2,1)} %bitcast.21) | data formatting | bytes 7864320
  115.6 0.0 copy-done.1
  115.6 13.8 %convert_bitcast_fusion = bf16[48,8,64,4,128]{4,2,1,0,3:T(8,128)(2,1)} fusion(bf16[48,8,40,128]{3,2,0,1:T(8,128)(2,1)} %bitcast.41, bf16[64,4]{0,1:T(4,128)(2,1)S(1)} %fusion.23, s32[64,4]{0,1:T(4,128)S(1)} %bitcast.44), kind=kOutput, calls=%fused_computation.2 | convolution fusion | flops 1019236352 | bytes 29099520 | tf_op jit(solution)/shard_map/...ta,skt->...ska/dot_general | solution.py:18
  129.4 59.8 %fusion.10 = bf16[64,48,1,8,128]{4,3,2,1,0:T(8,128)(2,1)} fusion(bf16[64,1,4,128,128]{4,3,2,1,0:T(8,128)(2,1)} %param.7, bf16[48,8,64,4,128]{4,2,1,0,3:T(8,128)(2,1)} %convert_bitcast_fusion), kind=kOutput, calls=%fused_computation.18 | convolution fusion | flops 3224371200 | bytes 39845888 | tf_op jit(solution)/shard_map/...ska,skab->...sb/dot_general | solution.py:21
  189.2 7.2 %copy.41 = bf16[64,48,1,8,128]{4,3,0,2,1:T(8,128)(2,1)} copy(bf16[64,48,1,8,128]{4,3,2,1,0:T(8,128)(2,1)} %fusion.10) | data formatting | bytes 12582912 | tf_op jit(solution)/shard_map/convert_element_type | solution.py:40
  196.5 0.0 copy-start
  196.5 0.0 reduce-scatter.2.cloned.1.call-update
  196.5 1.9 copy-done
  198.3 0.5 reduce_max.14
  198.9 35.2 %pmax.7 = f32[24,8]{1,0:T(8,128)S(1)} all-reduce(bf16[24,8]{1,0:T(8,128)(2,1)S(1)} %reduce_max.14), channel_id=1, replica_groups=mesh['groups'=2,'tok'=8,'voc'=2] {'tok'}, use_global_device_ids=true, to_apply=%region_1.0 | all-reduce | flops 192 | bytes 1152 | tf_op jit(solution)/shard_map/pmax | solution.py:47
  234.1 0.0 reduce-scatter.2.cloned.1.call-done
  234.1 4.8 %fusion.8 = (f32[24,8]{1,0:T(8,128)S(1)}, f32[24,8]{1,0:T(8,128)S(1)}, f32[24,8]{1,0:T(8,128)S(1)}, f32[24,8]{1,0:T(8,128)S(1)}) fusion(bf16[24,8,8192]{2,1,0:T(8,128)(2,1)} %reduce-scatter.2.cloned.1.call-done, bf16[24,8,8192]{2,1,0:T(8,128)(2,1)S(1)} %copy-done, f32[24,8]{1,0:T(8,128)S(1)} %pmax.7), kind=kLoop, calls=%fused_computation.16 | loop fusion | flops 14155008 | bytes 6295296 | tf_op jit(solution)/shard_map/reduce_sum | solution.py:45
  238.9 33.5 %all-reduce = (f32[24,8]{1,0:T(8,128)S(1)}, f32[24,8]{1,0:T(8,128)S(1)}, f32[24,8]{1,0:T(8,128)S(1)}, f32[24,8]{1,0:T(8,128)S(1)}) all-reduce(f32[24,8]{1,0:T(8,128)S(1)} %get-tuple-element.9, f32[24,8]{1,0:T(8,128)S(1)} %get-tuple-element.8, f32[24,8]{1,0:T(8,128)S(1)} %get-tuple-element.7, ...), channel_id=1, replica_groups=mesh['groups'=2,'tok'=8,'voc'=2] {'tok'}, use_global_device_ids=true, to_apply=%region_6.0 | all-reduce | flops 768 | bytes 6144 | tf_op jit(solution)/shard_map/psum | solution.py:49
  272.4 0.7 copy.24
  273.1 4.7 %fusion.11 = bf16[24,8,8192]{2,1,0:T(8,128)(2,1)} fusion(bf16[24,8,8192]{2,1,0:T(8,128)(2,1)} %reduce-scatter.2.cloned.1.call-done, bf16[24,8,8192]{2,1,0:T(8,128)(2,1)S(1)} %copy-done, f32[24,8]{1,0:T(8,128)S(1)} %get-tuple-element.10, f32[24,8]{1,0:T(8,128)S(1)} %get-tuple-element.11, f32[24,8]{1,0:T(8,128)S(1)} %pmax.7), kind=kLoop, calls=%fused_computation.20 | loop fusion | flops 12582912 | bytes 9439488 | tf_op jit(solution)/shard_map/convert_element_type | solution.py:56
  (2 shorter events, 0.0 us)
Async XLA Ops:
  11.4 11.5 %copy-start.2 = (s32[64,1]{0,1:T(1,128)S(1)}, s32[64,1]{0,1:T(1,128)}, u32[]{:S(2)}) copy-start(s32[64,1]{0,1:T(1,128)} %param.9) | copy-start | bytes 772
  15.5 100.1 %copy-start.1 = (s32[64,1,4]{0,2,1:T(4,128)S(1)}, s32[64,1,4]{0,2,1:T(4,128)}, u32[]{:S(2)}) copy-start(s32[64,1,4]{0,2,1:T(4,128)} %param.8) | copy-start | bytes 3076
  15.5 95.1 %all-to-all-start = ((bf16[48,8,5120]{2,0,1:T(8,128)(2,1)}), bf16[48,8,5120]{2,0,1:T(8,128)(2,1)}, u32[]{:S(2)}, u32[]{:S(2)}) async-start(bf16[48,8,5120]{2,0,1:T(8,128)(2,1)} %copy.20), calls=%async_computation | async-start | bytes 7864320 | tf_op jit(solution)/shard_map/all_to_all | solution.py:33
  22.9 211.2 %reduce-scatter.2.cloned.1.call-start = ((), (), s32[]{:S(2)}) async-start(), calls=%async_computation.2 | async-start | bytes 9437184 | tf_op jit(solution)/shard_map/reduce_scatter | solution.py:39
  196.5 1.9 copy-start
Sparse Core Ops, SparseCore 0:
  196.6 13.5 reduce-scatter.1
where the time goes:
time: 285 us
  waiting for transfers between devices  87.6 us (31%)
  matrix products  73.7 us (26%)
  blocking collectives  68.6 us (24%)
  local copies, waits for them, and re-layouts  23.1 us (8%)
  between operations  14.1 us (5%)
  other arithmetic  10 us (4%)
  starting transfers between devices  7.42 us (3%)
    all_to_all x1, waiting for transfers between devices, body(): lax.all_to_all(local_rows, 'tok', split_axis=1, concat_axis=1, tiled=True)  87.6 us
    dot_general x1, matrix products, apply_maps(): jnp.einsum('...ska,skab->...sb', picked, matrices, preferred_element_type...  59.8 us
    pmax x1, blocking collectives, body(): row_top = lax.pmax(local_top, 'tok')  35.2 us
    psum x1, blocking collectives, body(): lax.psum((jnp.sum(shifted, axis=-1), mass_local, entropy_local, cross_loc...  33.5 us
    dot_general x1, matrix products, apply_maps(): jnp.einsum('...ta,skt->...ska', split_cols, onehot, preferred_element_typ...  13.8 us
    unnamed x9, local copies, waits for them, and re-layouts  11.8 us
    all_to_all x1, starting transfers between devices, body(): lax.all_to_all(local_rows, 'tok', split_axis=1, concat_axis=1, tiled=True)  7.38 us
    convert_element_type x1, local copies, waits for them, and re-layouts, body(): partial_map.astype(jnp.bfloat16)  7.23 us
  transfers between devices with their start and end apart: 2, of which 1 were waited for; matrix products, arithmetic and copies ran while one was open for 0% of the time, Pallas kernels for 0%

commit v1 on v0

v1 whole, which is shorter than its diff:
```python
import functools

import jax
import jax.numpy as jnp
from jax import lax
from jax.experimental import pallas as pl
from jax.experimental.pallas import tpu as pltpu
from jax.sharding import PartitionSpec as P

MESH = pl.DeviceIdType.MESH
LANES = 128
FIELDS = 8
WINDOW = 3


def kernel(
    n, words, teacher, student_hbm, maps_hbm, slots, grad, div,
    cols, work, maps, student, part, other_part, stats, gathered,
    local_sem, send_sem, recv_sem, half_send, half_recv, stat_send, stat_recv,
):
    rows = cols.shape[1]
    span = cols.shape[2]
    teacher_blocks = span // LANES
    student_blocks = maps.shape[0]
    slots_all = maps.shape[1] // LANES
    half_rows = student.shape[1]
    width = student.shape[2]
    lanes = stats.shape[1]
    chunk = 512
    me = lax.axis_index("tok")
    voc = lax.axis_index("voc")
    other = 1 - voc

    def shift_of(step):
        near = (step + 1) // 2
        return n // 2 + (1 - 2 * lax.rem(step, 2)) * near

    def column_copy(step):
        target = lax.rem(me + shift_of(step), n)
        return pltpu.make_async_remote_copy(
            src_ref=teacher.at[:, pl.ds(pl.multiple_of(target * span, LANES), span)],
            dst_ref=cols.at[step + 1],
            send_sem=send_sem.at[step],
            recv_sem=recv_sem.at[step],
            device_id={"tok": target},
            device_id_type=MESH,
        )

    def half_copy(source):
        return pltpu.make_async_remote_copy(
            src_ref=part.at[source, pl.ds(pl.multiple_of(other * half_rows, 8), half_rows)],
            dst_ref=other_part.at[source],
            send_sem=half_send.at[source],
            recv_sem=half_recv.at[source],
            device_id={"voc": other},
            device_id_type=MESH,
        )

    def stat_copy(step):
        target = lax.rem(me + step + 1, n)
        return pltpu.make_async_remote_copy(
            src_ref=stats,
            dst_ref=gathered.at[step],
            send_sem=stat_send.at[step],
            recv_sem=stat_recv.at[step],
            device_id={"tok": target},
            device_id_type=MESH,
        )

    own_copy = pltpu.make_async_copy(
        teacher.at[:, pl.ds(pl.multiple_of(me * span, LANES), span)], cols.at[0], local_sem.at[0]
    )
    maps_copy = pltpu.make_async_copy(maps_hbm, maps, local_sem.at[1])
    student_copy = pltpu.make_async_copy(student_hbm, student, local_sem.at[2])
    own_copy.start()
    maps_copy.start()
    student_copy.start()

    barrier = pltpu.get_barrier_semaphore()

    @pl.loop(1, n)
    def _(step):
        pl.semaphore_signal(
            barrier, inc=1, device_id={"tok": lax.rem(me + step, n)}, device_id_type=MESH
        )

    pl.semaphore_signal(barrier, inc=1, device_id={"voc": other}, device_id_type=MESH)
    pl.semaphore_wait(barrier, n)

    for step in range(min(WINDOW, n - 1)):
        column_copy(step).start()

    work[teacher_blocks] = jnp.zeros((rows, LANES), work.dtype)
    stats[...] = jnp.zeros_like(stats)
    lane = lax.broadcasted_iota(jnp.int32, (half_rows, lanes), 1)

    def map_rows(slot, source):
        for block in range(teacher_blocks):
            work[block] = cols[slot, :, block * LANES : (block + 1) * LANES]

        @pl.loop(0, student_blocks, unroll=4)
        def _(block):
            picked = jnp.concatenate(
                [work[slots[block * slots_all + k]] for k in range(slots_all)], axis=1
            )
            part[source, :, pl.ds(pl.multiple_of(block * LANES, LANES), LANES)] = jnp.dot(
                picked, maps[block], preferred_element_type=jnp.float32
            )

        half_copy(source).start()

    def fold(x):
        return functools.reduce(
            lambda a, b: a + b, [x[:, c : c + LANES] for c in range(0, chunk, LANES)]
        )

    def mapped_of(source, at):
        mine = part[source, pl.ds(pl.multiple_of(voc * half_rows, 8), half_rows), at]
        return mine + other_part[source, :, at]

    def row_stats(source):
        def top_step(c, top):
            at = pl.ds(pl.multiple_of(c * chunk, chunk), chunk)
            x = student[source, :, at].astype(jnp.float32)
            for k in range(0, chunk, LANES):
                top = jnp.maximum(top, x[:, k : k + LANES])
            return top

        start = jnp.full((half_rows, LANES), -jnp.inf, jnp.float32)
        top = jnp.max(
            lax.fori_loop(0, width // chunk, top_step, start), axis=1, keepdims=True
        )
        half_copy(source).wait()

        def sum_step(c, sums):
            at = pl.ds(pl.multiple_of(c * chunk, chunk), chunk)
            x = student[source, :, at].astype(jnp.float32)
            mapped = mapped_of(source, at)
            terms = (jnp.exp(x - top), mapped, mapped * jnp.log(mapped), mapped * x)
            return tuple(s + fold(t) for s, t in zip(sums, terms))

        zero = jnp.zeros((half_rows, LANES), jnp.float32)
        sums = lax.fori_loop(0, width // chunk, sum_step, (zero,) * 4)
        packed = stats[...]
        values = (top,) + tuple(jnp.sum(s, axis=1, keepdims=True) for s in sums)
        for field, value in enumerate(values):
            packed = jnp.where(lane == source * FIELDS + field, value, packed)
        stats[...] = packed

    own_copy.wait()
    maps_copy.wait()
    map_rows(0, me)
    student_copy.wait()

    def source_of(step):
        return lax.rem(me - shift_of(step) + n, n)

    @pl.loop(0, n - 1)
    def _(step):
        column_copy(step).wait()

        @pl.when(step + WINDOW < n - 1)
        def _():
            column_copy(step + WINDOW).start()

        map_rows(step + 1, source_of(step))
        row_stats(lax.select(step == 0, me, source_of(jnp.maximum(step - 1, 0))))

    row_stats(source_of(n - 2))

    @pl.loop(0, n - 1)
    def _(step):
        stat_copy(step).start()

    @pl.loop(0, n - 1)
    def _(step):
        stat_copy(step).wait()

    own = stats[...]
    top = lax.fori_loop(0, n - 1, lambda d, t: jnp.maximum(t, gathered[d]), own)
    is_exp = lax.rem(lane, FIELDS) == 1

    def scaled(g):
        return jnp.where(is_exp, g * jnp.exp(pltpu.roll(g - top, 1, 1)), g)

    total = lax.fori_loop(0, n - 1, lambda d, t: t + scaled(gathered[d]), scaled(own))
    exp_total, mass, entropy, cross = (pltpu.roll(total, lanes - k, 1) for k in (1, 2, 3, 4))
    div[...] = entropy / mass - jnp.log(mass) - cross / mass + top + jnp.log(exp_total)
    exp_scale = words / exp_total
    map_scale = words / mass

    @pl.loop(0, n)
    def _(source):
        here = lane == source * FIELDS
        row_top, row_exp, row_map = (
            jnp.sum(jnp.where(here, v, 0.0), axis=1, keepdims=True)
            for v in (top, exp_scale, map_scale)
        )

        @pl.loop(0, width // chunk)
        def _(c):
            at = pl.ds(pl.multiple_of(c * chunk, chunk), chunk)
            x = student[source, :, at].astype(jnp.float32)
            value = jnp.exp(x - row_top) * row_exp - mapped_of(source, at) * row_map
            grad[source, :, at] = value.astype(grad.dtype)


def body(teacher, student, block_maps, slot_index, slot_count):
    n = lax.axis_size("tok")
    rows = teacher.shape[1]
    half_rows, _, width = student.shape
    student_blocks, _, slots_all, depth, block = block_maps.shape
    span = teacher.shape[2] // n
    teacher_blocks = span // block
    lanes = max(LANES, n * FIELDS)
    used = jnp.arange(slots_all, dtype=jnp.int32)[None, :] < slot_count[:, :1]
    slots = jnp.where(used, slot_index[:, 0], teacher_blocks).reshape(-1)
    anywhere = pl.BlockSpec(memory_space=pl.ANY)
    in_vmem = pl.BlockSpec(memory_space=pltpu.VMEM)
    dma = pltpu.SemaphoreType.DMA
    grad, div = pl.pallas_call(
        functools.partial(kernel, n, float(n * width)),
        out_shape=(
            jax.ShapeDtypeStruct((n, half_rows, width), jnp.bfloat16),
            jax.ShapeDtypeStruct((half_rows, lanes), jnp.float32),
        ),
        in_specs=[anywhere, anywhere, anywhere, pl.BlockSpec(memory_space=pltpu.SMEM)],
        out_specs=(in_vmem, in_vmem),
        scratch_shapes=[
            pltpu.VMEM((n, rows, span), jnp.bfloat16),
            pltpu.VMEM((teacher_blocks + 1, rows, block), jnp.bfloat16),
            pltpu.VMEM((student_blocks, slots_all * depth, block), jnp.bfloat16),
            pltpu.VMEM((n, half_rows, width), jnp.bfloat16),
            pltpu.VMEM((n, rows, width), jnp.float32),
            pltpu.VMEM((n, half_rows, width), jnp.float32),
            pltpu.VMEM((half_rows, lanes), jnp.float32),
            pltpu.VMEM((n - 1, half_rows, lanes), jnp.float32),
            dma((3,)),
            dma((n - 1,)),
            dma((n - 1,)),
            dma((n,)),
            dma((n,)),
            dma((n - 1,)),
            dma((n - 1,)),
        ],
        compiler_params=pltpu.CompilerParams(
            collective_id=0, has_side_effects=True, vmem_limit_bytes=56 * 2**20
        ),
    )(
        teacher[0],
        jnp.swapaxes(student, 0, 1),
        block_maps.reshape(student_blocks, slots_all * depth, block),
        slots,
    )
    divergence = div.reshape(half_rows, -1, FIELDS)[:, :n, 0]
    return jnp.swapaxes(grad, 0, 1), divergence


def solution(mesh):
    return jax.shard_map(
        body,
        mesh=mesh,
        in_specs=(
            P(("groups", "tok"), None, "voc"),
            P("voc", "groups", "tok"),
            P("tok", "voc", None, None, None),
            P("tok", "voc", None),
            P("tok", "voc"),
        ),
        out_specs=(P("voc", "groups", "tok"), P("voc", "groups")),
        check_vma=False,
    )
```

time: 285 us -> 134 us (0.47)
  Pallas kernels: 0 us -> 120 us
  waiting for transfers between devices: 87.6 us -> 0 us
  matrix products: 73.7 us -> 0 us
  blocking collectives: 68.6 us -> 0 us
  between operations: 14.1 us -> 0.66 us
  local copies, waits for them, and re-layouts: 23.1 us -> 12.3 us
  other arithmetic: 10 us -> 1.3 us
  starting transfers between devices: 7.42 us -> 0 us
    pallas_call x0 -> x1, Pallas kernels: none -> 120 us  [body(): pl.pallas_call(functools.partial(kernel, n, float(n * width)), out_shape=...]
    all_to_all x1 -> x0, waiting for transfers between devices: 87.6 us -> none  [body(): lax.all_to_all(local_rows, 'tok', split_axis=1, concat_axis=1, tiled=True)]
    dot_general x2 -> x0, matrix products: 73.7 us -> none  [the longest x1 59.8 us: apply_maps(): jnp.einsum('...ska,skab->...sb', picked, matrices, preferred_element_type...]
    pmax x1 -> x0, blocking collectives: 35.2 us -> none  [body(): row_top = lax.pmax(local_top, 'tok')]
    psum x1 -> x0, blocking collectives: 33.5 us -> none  [body(): lax.psum((jnp.sum(shifted, axis=-1), mass_local, entropy_local, cross_loc...]
    all_to_all x1 -> x0, starting transfers between devices: 7.38 us -> none  [body(): lax.all_to_all(local_rows, 'tok', split_axis=1, concat_axis=1, tiled=True)]
    convert_element_type x1 -> x0, local copies, waits for them, and re-layouts: 7.23 us -> none  [body(): partial_map.astype(jnp.bfloat16)]
    reduce_sum x1 -> x0, other arithmetic: 4.84 us -> none  [body(): entropy_local = jnp.sum(mapped * jnp.log(mapped), axis=-1)]
  transfers between devices with their start and end apart: 2 -> 0, of which waited for: 1 -> 0; matrix products, arithmetic and copies ran while one was open for 0% -> 0% of each run, Pallas kernels for 0% -> 0%
where the time goes in v1:
time: 134 us
  Pallas kernels  120 us (90%)
  local copies, waits for them, and re-layouts  12.3 us (9%)
    pallas_call x1, Pallas kernels, body(): pl.pallas_call(functools.partial(kernel, n, float(n * width)), out_shape=...  120 us
    unnamed x5, local copies, waits for them, and re-layouts  11.4 us

profile of v1, /device:TPU:0, one launch (start us, length us, event | category | flops | bytes accessed | tf_op | source)
XLA Modules:
  0.0 133.8 jit_solution(8973138539544440485)
XLA Ops:
  0.6 0.7 iota_compare_fusion
  1.4 0.1 lt.23
  1.5 0.8 copy.11
  2.3 0.1 squeeze.10
  2.4 0.6 broadcast_select_fusion.slots
  2.9 5.3 %copy.15 = bf16[24,8,8192]{2,0,1:T(8,128)(2,1)} copy(bf16[24,8,8192]{2,1,0:T(8,128)(2,1)} %param.6) | data formatting | bytes 6291456 | tf_op args[1]
  8.2 119.6 %shard_map.68 = (bf16[8,24,8192]{2,1,0:T(8,128)(2,1)}, f32[24,128]{1,0:T(8,128)}) custom-call(bf16[48,40960]{1,0:T(8,128)(2,1)} %bitcast.13, bf16[8,24,8192]{2,1,0:T(8,128)(2,1)} %bitcast.11, bf16[64,512,128]{2,1,0:T(8,128)(2,1)} %bitcast.12, s32[256]{0:T(256)} %broadcast_select_fusion.slots), custom_call_target="tpu_custom_call" | custom-call | tf_op jit(solution)/shard_map/pallas_call | solution.py:221
  127.8 0.0 copy-start
  127.8 5.3 %copy.13 = bf16[24,8,8192]{2,1,0:T(8,128)(2,1)} copy(bf16[24,8,8192]{2,0,1:T(8,128)(2,1)} %bitcast.14) | data formatting | bytes 6291456
  133.1 0.0 copy-done
  133.1 0.1 copy.12
  133.2 0.6 slice.4
Async XLA Ops:
  127.8 5.3 %copy-start = (f32[24,128]{1,0:T(8,128)S(1)}, f32[24,128]{1,0:T(8,128)}, u32[]{:S(2)}) copy-start(f32[24,128]{1,0:T(8,128)} %get-tuple-element.5) | copy-start | bytes 36868

commit v2 on v1

--- a/solution.py
+++ b/solution.py
@@ -10,7 +10,7 @@
 MESH = pl.DeviceIdType.MESH
 LANES = 128
 FIELDS = 8
-WINDOW = 3
+WINDOW = 4
 
 
 def kernel(
@@ -31,12 +31,20 @@
     voc = lax.axis_index("voc")
     other = 1 - voc
 
-    def shift_of(step):
-        near = (step + 1) // 2
-        return n // 2 + (1 - 2 * lax.rem(step, 2)) * near
+    def partner(step):
+        half = (step + 1) // 2
+        odd = lax.rem(step, 2)
+        mask = odd * half + (1 - odd) * (n - 1 - half)
+        total, bit = 0, 1
+        while bit < n:
+            mine = lax.rem(me // bit, 2)
+            flip = lax.rem(mask // bit, 2)
+            total = total + bit * (mine + flip - 2 * mine * flip)
+            bit *= 2
+        return total
 
     def column_copy(step):
-        target = lax.rem(me + shift_of(step), n)
+        target = partner(step)
         return pltpu.make_async_remote_copy(
             src_ref=teacher.at[:, pl.ds(pl.multiple_of(target * span, LANES), span)],
             dst_ref=cols.at[step + 1],
@@ -153,7 +161,7 @@
     student_copy.wait()
 
     def source_of(step):
-        return lax.rem(me - shift_of(step) + n, n)
+        return partner(step)
 
     @pl.loop(0, n - 1)
     def _(step):

time: 134 us -> 124 us (0.925)
  Pallas kernels: 120 us -> 109 us
    pallas_call x1, Pallas kernels: 120 us -> 109 us  [body(): pl.pallas_call(functools.partial(kernel, n, float(n * width)), out_shape=...]
where the time goes in v2:
time: 124 us; the launch traced here: 123 us
  Pallas kernels  109 us (88%)
  local copies, waits for them, and re-layouts  12.3 us (10%)
  other arithmetic  1.3 us (1%)
    pallas_call x1, Pallas kernels, body(): pl.pallas_call(functools.partial(kernel, n, float(n * width)), out_shape=...  109 us
    unnamed x5, local copies, waits for them, and re-layouts  11.4 us

profile of v2, /device:TPU:0, one launch (start us, length us, event | category | flops | bytes accessed | tf_op | source)
XLA Modules:
  0.0 123.4 jit_solution(10497874243252605925)
XLA Ops:
  0.6 0.7 iota_compare_fusion
  1.4 0.1 lt.23
  1.5 0.8 copy.11
  2.3 0.1 squeeze.10
  2.4 0.6 broadcast_select_fusion.slots
  2.9 5.3 %copy.15 = bf16[24,8,8192]{2,0,1:T(8,128)(2,1)} copy(bf16[24,8,8192]{2,1,0:T(8,128)(2,1)} %param.6) | data formatting | bytes 6291456 | tf_op args[1]
  8.2 109.2 %shard_map.68 = (bf16[8,24,8192]{2,1,0:T(8,128)(2,1)}, f32[24,128]{1,0:T(8,128)}) custom-call(bf16[48,40960]{1,0:T(8,128)(2,1)} %bitcast.13, bf16[8,24,8192]{2,1,0:T(8,128)(2,1)} %bitcast.11, bf16[64,512,128]{2,1,0:T(8,128)(2,1)} %bitcast.12, s32[256]{0:T(256)} %broadcast_select_fusion.slots), custom_call_target="tpu_custom_call" | custom-call | tf_op jit(solution)/shard_map/pallas_call | solution.py:229
  117.4 0.0 copy-start
  117.4 5.3 %copy.13 = bf16[24,8,8192]{2,1,0:T(8,128)(2,1)} copy(bf16[24,8,8192]{2,0,1:T(8,128)(2,1)} %bitcast.14) | data formatting | bytes 6291456
  122.7 0.0 copy-done
  122.7 0.1 copy.12
  122.8 0.6 slice.4
Async XLA Ops:
  117.4 5.3 %copy-start = (f32[24,128]{1,0:T(8,128)S(1)}, f32[24,128]{1,0:T(8,128)}, u32[]{:S(2)}) copy-start(f32[24,128]{1,0:T(8,128)} %get-tuple-element.5) | copy-start | bytes 36868

commit v3 on v2

--- a/solution.py
+++ b/solution.py
@@ -14,8 +14,8 @@
 
 
 def kernel(
-    n, words, teacher, student_hbm, maps_hbm, slots, grad, div,
-    cols, work, maps, student, part, other_part, stats, gathered,
+    n, words, teacher, student_hbm, maps_hbm, slots, counts, grad, div,
+    cols, work, maps, student, part, other_part, logits, mapped_all, scales, stats, gathered,
     local_sem, send_sem, recv_sem, half_send, half_recv, stat_send, stat_recv,
 ):
     rows = cols.shape[1]
@@ -23,7 +23,7 @@
     teacher_blocks = span // LANES
     student_blocks = maps.shape[0]
     slots_all = maps.shape[1] // LANES
-    half_rows = student.shape[1]
+    half_rows = student.shape[0]
     width = student.shape[2]
     lanes = stats.shape[1]
     chunk = 512
@@ -109,7 +109,11 @@
         @pl.loop(0, student_blocks, unroll=4)
         def _(block):
             picked = jnp.concatenate(
-                [work[slots[block * slots_all + k]] for k in range(slots_all)], axis=1
+                [
+                    work[lax.select(k < counts[block], slots[block, k], teacher_blocks)]
+                    for k in range(slots_all)
+                ],
+                axis=1,
             )
             part[source, :, pl.ds(pl.multiple_of(block * LANES, LANES), LANES)] = jnp.dot(
                 picked, maps[block], preferred_element_type=jnp.float32
@@ -117,21 +121,17 @@
 
         half_copy(source).start()
 
-    def fold(x):
-        return functools.reduce(
-            lambda a, b: a + b, [x[:, c : c + LANES] for c in range(0, chunk, LANES)]
-        )
-
     def mapped_of(source, at):
         mine = part[source, pl.ds(pl.multiple_of(voc * half_rows, 8), half_rows), at]
         return mine + other_part[source, :, at]
 
+    def shard_rows(source):
+        return pl.ds(source, half_rows, stride=n)
+
     def row_stats(source):
         def top_step(c, top):
-            at = pl.ds(pl.multiple_of(c * chunk, chunk), chunk)
-            x = student[source, :, at].astype(jnp.float32)
-            for k in range(0, chunk, LANES):
-                top = jnp.maximum(top, x[:, k : k + LANES])
+            for k in range(chunk // LANES):
+                top = jnp.maximum(top, logits[c * (chunk // LANES) + k, shard_rows(source), :])
             return top
 
         start = jnp.full((half_rows, LANES), -jnp.inf, jnp.float32)
@@ -141,11 +141,16 @@
         half_copy(source).wait()
 
         def sum_step(c, sums):
-            at = pl.ds(pl.multiple_of(c * chunk, chunk), chunk)
-            x = student[source, :, at].astype(jnp.float32)
-            mapped = mapped_of(source, at)
-            terms = (jnp.exp(x - top), mapped, mapped * jnp.log(mapped), mapped * x)
-            return tuple(s + fold(t) for s, t in zip(sums, terms))
+            for k in range(chunk // LANES):
+                block = c * (chunk // LANES) + k
+                x = logits[block, shard_rows(source), :]
+                mapped = mapped_of(source, pl.ds(pl.multiple_of(block * LANES, LANES), LANES))
+                shifted = jnp.exp(x - top)
+                logits[block, shard_rows(source), :] = shifted
+                mapped_all[block, shard_rows(source), :] = mapped
+                terms = (shifted, mapped, mapped * jnp.log(mapped), mapped * x)
+                sums = tuple(s + v for s, v in zip(sums, terms))
+            return sums
 
         zero = jnp.zeros((half_rows, LANES), jnp.float32)
         sums = lax.fori_loop(0, width // chunk, sum_step, (zero,) * 4)
@@ -160,6 +165,12 @@
     map_rows(0, me)
     student_copy.wait()
 
+    @pl.loop(0, half_rows)
+    def _(row):
+        at = pl.ds(pl.multiple_of(row * n, 8), n)
+        for c in range(width // LANES):
+            logits[c, at, :] = student[row, :, c * LANES : (c + 1) * LANES].astype(jnp.float32)
+
     def source_of(step):
         return partner(step)
 
@@ -194,23 +205,23 @@
     total = lax.fori_loop(0, n - 1, lambda d, t: t + scaled(gathered[d]), scaled(own))
     exp_total, mass, entropy, cross = (pltpu.roll(total, lanes - k, 1) for k in (1, 2, 3, 4))
     div[...] = entropy / mass - jnp.log(mass) - cross / mass + top + jnp.log(exp_total)
-    exp_scale = words / exp_total
+    exp_scale = jnp.exp(own - top) * (words / exp_total)
     map_scale = words / mass
 
     @pl.loop(0, n)
     def _(source):
         here = lane == source * FIELDS
-        row_top, row_exp, row_map = (
-            jnp.sum(jnp.where(here, v, 0.0), axis=1, keepdims=True)
-            for v in (top, exp_scale, map_scale)
-        )
-
-        @pl.loop(0, width // chunk)
-        def _(c):
-            at = pl.ds(pl.multiple_of(c * chunk, chunk), chunk)
-            x = student[source, :, at].astype(jnp.float32)
-            value = jnp.exp(x - row_top) * row_exp - mapped_of(source, at) * row_map
-            grad[source, :, at] = value.astype(grad.dtype)
+        for which, value in enumerate((exp_scale, map_scale)):
+            column = jnp.sum(jnp.where(here, value, 0.0), axis=1, keepdims=True)
+            scales[which, shard_rows(source), :] = jnp.broadcast_to(column, (half_rows, LANES))
+
+    @pl.loop(0, half_rows)
+    def _(row):
+        at = pl.ds(pl.multiple_of(row * n, 8), n)
+        row_exp, row_map = scales[0, at, :], scales[1, at, :]
+        for c in range(width // LANES):
+            value = logits[c, at, :] * row_exp - mapped_all[c, at, :] * row_map
+            grad[row, :, c * LANES : (c + 1) * LANES] = value.astype(grad.dtype)
 
 
 def body(teacher, student, block_maps, slot_index, slot_count):
@@ -221,26 +232,27 @@
     span = teacher.shape[2] // n
     teacher_blocks = span // block
     lanes = max(LANES, n * FIELDS)
-    used = jnp.arange(slots_all, dtype=jnp.int32)[None, :] < slot_count[:, :1]
-    slots = jnp.where(used, slot_index[:, 0], teacher_blocks).reshape(-1)
     anywhere = pl.BlockSpec(memory_space=pl.ANY)
     in_vmem = pl.BlockSpec(memory_space=pltpu.VMEM)
     dma = pltpu.SemaphoreType.DMA
     grad, div = pl.pallas_call(
         functools.partial(kernel, n, float(n * width)),
         out_shape=(
-            jax.ShapeDtypeStruct((n, half_rows, width), jnp.bfloat16),
+            jax.ShapeDtypeStruct((half_rows, n, width), jnp.bfloat16),
             jax.ShapeDtypeStruct((half_rows, lanes), jnp.float32),
         ),
-        in_specs=[anywhere, anywhere, anywhere, pl.BlockSpec(memory_space=pltpu.SMEM)],
+        in_specs=[anywhere] * 3 + [pl.BlockSpec(memory_space=pltpu.SMEM)] * 2,
         out_specs=(in_vmem, in_vmem),
         scratch_shapes=[
             pltpu.VMEM((n, rows, span), jnp.bfloat16),
             pltpu.VMEM((teacher_blocks + 1, rows, block), jnp.bfloat16),
             pltpu.VMEM((student_blocks, slots_all * depth, block), jnp.bfloat16),
-            pltpu.VMEM((n, half_rows, width), jnp.bfloat16),
+            pltpu.VMEM((half_rows, n, width), jnp.bfloat16),
             pltpu.VMEM((n, rows, width), jnp.float32),
             pltpu.VMEM((n, half_rows, width), jnp.float32),
+            pltpu.VMEM((width // LANES, half_rows * n, LANES), jnp.float32),
+            pltpu.VMEM((width // LANES, half_rows * n, LANES), jnp.float32),
+            pltpu.VMEM((2, half_rows * n, LANES), jnp.float32),
             pltpu.VMEM((half_rows, lanes), jnp.float32),
             pltpu.VMEM((n - 1, half_rows, lanes), jnp.float32),
             dma((3,)),
@@ -252,16 +264,17 @@
             dma((n - 1,)),
         ],
         compiler_params=pltpu.CompilerParams(
-            collective_id=0, has_side_effects=True, vmem_limit_bytes=56 * 2**20
+            collective_id=0, has_side_effects=True, vmem_limit_bytes=60 * 2**20
         ),
     )(
         teacher[0],
-        jnp.swapaxes(student, 0, 1),
+        student,
         block_maps.reshape(student_blocks, slots_all * depth, block),
-        slots,
+        slot_index[:, 0],
+        slot_count[:, 0],
     )
     divergence = div.reshape(half_rows, -1, FIELDS)[:, :n, 0]
-    return jnp.swapaxes(grad, 0, 1), divergence
+    return grad, divergence
 
 
 def solution(mesh):

time: 124 us -> 117 us (0.944)
  local copies, waits for them, and re-layouts: 12.3 us -> 6.64 us
  other arithmetic: 1.3 us -> 0 us
    unnamed x5 -> x2, local copies, waits for them, and re-layouts: 11.4 us -> 5.24 us
where the time goes in v3:
time: 117 us
  Pallas kernels  109 us (93%)
  local copies, waits for them, and re-layouts  6.64 us (6%)
    pallas_call x1, Pallas kernels, body(): pl.pallas_call(functools.partial(kernel, n, float(n * width)), out_shape=...  109 us
    unnamed x2, local copies, waits for them, and re-layouts  5.24 us

profile of v3, /device:TPU:0, one launch (start us, length us, event | category | flops | bytes accessed | tf_op | source)
XLA Modules:
  0.0 116.7 jit_solution(15351828995838324805)
XLA Ops:
  0.6 1.4 %copy.9 = s32[64,1,4]{2,0,1:T(8,128)} copy(s32[64,1,4]{0,2,1:T(4,128)} %param.8) | data formatting | bytes 2048 | tf_op args[3]
  2.0 109.5 %shard_map.68 = (bf16[24,8,8192]{2,1,0:T(8,128)(2,1)}, f32[24,128]{1,0:T(8,128)}) custom-call(bf16[48,40960]{1,0:T(8,128)(2,1)} %bitcast.7, bf16[24,8,8192]{2,1,0:T(8,128)(2,1)} %student_hbm.1, bf16[64,512,128]{2,1,0:T(8,128)(2,1)} %bitcast.6, s32[64,4]{1,0:T(8,128)} %bitcast.8, s32[64]{0:T(128)} %bitcast.11), custom_call_target="tpu_custom_call" | custom-call | tf_op jit(solution)/shard_map/pallas_call | solution.py:238
  111.5 0.8 copy.10
  112.3 0.6 slice.4
  112.9 3.9 %copy.12 = bf16[24,8,8192]{2,1,0:T(8,128)(2,1)} copy(bf16[24,8,8192]{2,1,0:T(8,128)(2,1)} %get-tuple-element.8) | data formatting | bytes 6291456

commit v4 on v3

--- a/solution.py
+++ b/solution.py
@@ -10,7 +10,7 @@
 MESH = pl.DeviceIdType.MESH
 LANES = 128
 FIELDS = 8
-WINDOW = 4
+WINDOW = 7
 
 
 def kernel(
@@ -106,7 +106,7 @@
         for block in range(teacher_blocks):
             work[block] = cols[slot, :, block * LANES : (block + 1) * LANES]
 
-        @pl.loop(0, student_blocks, unroll=4)
+        @pl.loop(0, student_blocks, unroll=min(16, student_blocks))
         def _(block):
             picked = jnp.concatenate(
                 [
@@ -204,16 +204,21 @@
 
     total = lax.fori_loop(0, n - 1, lambda d, t: t + scaled(gathered[d]), scaled(own))
     exp_total, mass, entropy, cross = (pltpu.roll(total, lanes - k, 1) for k in (1, 2, 3, 4))
-    div[...] = entropy / mass - jnp.log(mass) - cross / mass + top + jnp.log(exp_total)
+    spread = entropy / mass - jnp.log(mass) - cross / mass + top + jnp.log(exp_total)
     exp_scale = jnp.exp(own - top) * (words / exp_total)
     map_scale = words / mass
 
-    @pl.loop(0, n)
-    def _(source):
+    div_lane = lax.broadcasted_iota(jnp.int32, (half_rows, n), 1)
+
+    def unpack(source, tokens):
         here = lane == source * FIELDS
         for which, value in enumerate((exp_scale, map_scale)):
             column = jnp.sum(jnp.where(here, value, 0.0), axis=1, keepdims=True)
             scales[which, shard_rows(source), :] = jnp.broadcast_to(column, (half_rows, LANES))
+        token = jnp.sum(jnp.where(here, spread, 0.0), axis=1, keepdims=True)
+        return jnp.where(div_lane == source, token, tokens)
+
+    div[...] = lax.fori_loop(0, n, unpack, jnp.zeros((half_rows, n), jnp.float32))
 
     @pl.loop(0, half_rows)
     def _(row):
@@ -239,7 +244,7 @@
         functools.partial(kernel, n, float(n * width)),
         out_shape=(
             jax.ShapeDtypeStruct((half_rows, n, width), jnp.bfloat16),
-            jax.ShapeDtypeStruct((half_rows, lanes), jnp.float32),
+            jax.ShapeDtypeStruct((half_rows, n), jnp.float32),
         ),
         in_specs=[anywhere] * 3 + [pl.BlockSpec(memory_space=pltpu.SMEM)] * 2,
         out_specs=(in_vmem, in_vmem),
@@ -273,8 +278,7 @@
         slot_index[:, 0],
         slot_count[:, 0],
     )
-    divergence = div.reshape(half_rows, -1, FIELDS)[:, :n, 0]
-    return grad, divergence
+    return grad, div
 
 
 def solution(mesh):

time: 117 us -> 114 us (0.974)
  Pallas kernels: 109 us -> 107 us
    pallas_call x1, Pallas kernels: 109 us -> 107 us  [body(): pl.pallas_call(functools.partial(kernel, n, float(n * width)), out_shape=...]
where the time goes in v4:
time: 114 us
  Pallas kernels  107 us (94%)
  local copies, waits for them, and re-layouts  6.61 us (6%)
    pallas_call x1, Pallas kernels, body(): pl.pallas_call(functools.partial(kernel, n, float(n * width)), out_shape=...  107 us
    unnamed x2, local copies, waits for them, and re-layouts  5.24 us

profile of v4, /device:TPU:0, one launch (start us, length us, event | category | flops | bytes accessed | tf_op | source)
XLA Modules:
  0.0 114.1 jit_solution(16819759202194829806)
XLA Ops:
  0.6 1.4 %copy.7 = s32[64,1,4]{2,0,1:T(8,128)} copy(s32[64,1,4]{0,2,1:T(4,128)} %param.8) | data formatting | bytes 2048 | tf_op args[3]
  2.0 106.9 %shard_map.68 = (bf16[24,8,8192]{2,1,0:T(8,128)(2,1)}, f32[24,8]{1,0:T(8,128)}) custom-call(bf16[48,40960]{1,0:T(8,128)(2,1)} %bitcast.5, bf16[24,8,8192]{2,1,0:T(8,128)(2,1)} %student_hbm.1, bf16[64,512,128]{2,1,0:T(8,128)(2,1)} %bitcast.4, s32[64,4]{1,0:T(8,128)} %bitcast.6, s32[64]{0:T(128)} %bitcast.7), custom_call_target="tpu_custom_call" | custom-call | tf_op jit(solution)/shard_map/pallas_call | solution.py:243
  108.9 1.4 %copy.8 = f32[24,8]{0,1:T(8,128)} copy(f32[24,8]{1,0:T(8,128)} %get-tuple-element.3) | data formatting | bytes 1536 | tf_op jit(solution)/shard_map/pallas_call | solution.py:243
  110.3 3.9 %copy.10 = bf16[24,8,8192]{2,1,0:T(8,128)(2,1)} copy(bf16[24,8,8192]{2,1,0:T(8,128)(2,1)} %get-tuple-element.6) | data formatting | bytes 6291456

commit v5 on v4

--- a/solution.py
+++ b/solution.py
@@ -26,7 +26,7 @@
     half_rows = student.shape[0]
     width = student.shape[2]
     lanes = stats.shape[1]
-    chunk = 512
+    chunk = 1024
     me = lax.axis_index("tok")
     voc = lax.axis_index("voc")
     other = 1 - voc

time: 114 us -> 114 us (level)
  no operation moved by 1% of the time
where the time goes in v5:
time: 114 us
  Pallas kernels  107 us (94%)
  local copies, waits for them, and re-layouts  6.61 us (6%)
    pallas_call x1, Pallas kernels, body(): pl.pallas_call(functools.partial(kernel, n, float(n * width)), out_shape=...  107 us
    unnamed x2, local copies, waits for them, and re-layouts  5.24 us

profile of v5, /device:TPU:0, one launch (start us, length us, event | category | flops | bytes accessed | tf_op | source)
XLA Modules:
  0.0 114.1 jit_solution(16144356262856013511)
XLA Ops:
  0.6 1.4 %copy.7 = s32[64,1,4]{2,0,1:T(8,128)} copy(s32[64,1,4]{0,2,1:T(4,128)} %param.8) | data formatting | bytes 2048 | tf_op args[3]
  2.0 106.8 %shard_map.68 = (bf16[24,8,8192]{2,1,0:T(8,128)(2,1)}, f32[24,8]{1,0:T(8,128)}) custom-call(bf16[48,40960]{1,0:T(8,128)(2,1)} %bitcast.5, bf16[24,8,8192]{2,1,0:T(8,128)(2,1)} %student_hbm.1, bf16[64,512,128]{2,1,0:T(8,128)(2,1)} %bitcast.4, s32[64,4]{1,0:T(8,128)} %bitcast.6, s32[64]{0:T(128)} %bitcast.7), custom_call_target="tpu_custom_call" | custom-call | tf_op jit(solution)/shard_map/pallas_call | solution.py:243
  108.8 1.4 %copy.8 = f32[24,8]{0,1:T(8,128)} copy(f32[24,8]{1,0:T(8,128)} %get-tuple-element.3) | data formatting | bytes 1536 | tf_op jit(solution)/shard_map/pallas_call | solution.py:243
  110.2 3.9 %copy.10 = bf16[24,8,8192]{2,1,0:T(8,128)(2,1)} copy(bf16[24,8,8192]{2,1,0:T(8,128)(2,1)} %get-tuple-element.6) | data formatting | bytes 6291456
